TPU v7x, 256 devices: a whole 4x4x8 slice. The times are simulated.
256 devices in a mesh: expert: 64 (over z, x, core), inner: 4 (over y).
Axes of the slice: x: 4, y: 4, z: 8, core: 2. Of those that a mesh axis runs over, the one named last changes fastest.
Arguments:
- tokens_one: bfloat16 [1024, 7168], P('expert', 'inner'), may hold values from -6 to 6
- experts_one: int32 [1024, 8], P('expert'), may hold values from 0 to 63, as said below
- gates_one: float32 [1024, 8], P('expert'), may hold values from 0.1 to 1
- tokens_two: bfloat16 [1024, 7168], P('expert', 'inner'), may hold values from -6 to 6
- experts_two: int32 [1024, 8], P('expert'), may hold values from 0 to 63, as said below
- gates_two: float32 [1024, 8], P('expert'), may hold values from 0.1 to 1
- replica_pick: int32 [1024, 8], P('expert'), may hold values from 0 to 839
- home: int32 [64], replicated, may hold values from 0 to 63, each once
- w_gate_up: bfloat16 [64, 2, 7168, 1024], P('expert', None, None, 'inner'), may hold values from -0.0625 to 0.0625
- w_down: bfloat16 [64, 1024, 7168], P('expert', 'inner'), may hold values from -0.1875 to 0.1875
Outputs:
- mixed_one: bfloat16 [1024, 7168], P('expert', 'inner')
- mixed_two: bfloat16 [1024, 7168], P('expert', 'inner')
Inputs may be any that keep to these rules, and one draw needn't show every extreme that they name: `experts_one`: each row names 8 different experts. `experts_two`: each row names 8 different experts.
All inputs are finite; a program needn't handle non-finite values.
Results may differ from a plain program's by a relative error of at most 0.0058.
Values may be sent and summed in bfloat16 or wider, within the bound.
A program may use at most 128 MiB of HBM per device.

v0:
```python
import jax
import jax.numpy as jnp
from jax import lax
from jax.sharding import PartitionSpec as P

TOPK = 8
COPIES = 3


def from_root(value, axis, source):
    kept = jnp.where(lax.axis_index(axis) == source, value, 0).astype(value.dtype)
    return lax.psum(kept, axis)


def tally_counts(length):
    return jnp.arange(length, dtype=jnp.int32)


def table_lookup(lookup_table, positions):
    matches = positions[..., None] == tally_counts(lookup_table.shape[0])
    return jnp.sum(jnp.where(matches, lookup_table, 0), axis=-1, dtype=jnp.int32)


def rank_within(keys, key_count):
    onehot = (keys[..., None] == tally_counts(key_count)).astype(jnp.int32)
    running = jnp.cumsum(onehot, axis=-2, dtype=jnp.int32)
    return jnp.sum(running * onehot, axis=-1, dtype=jnp.int32) - 1


def layout_from_demand(counts, home):
    experts = home.shape[0]
    hot_expert = jnp.argmax(counts)
    busiest_resident = table_lookup(home, hot_expert)
    numbers = tally_counts(COPIES) + 1
    offsets = numbers // 2 * (experts // 2) + numbers % 2
    copies = (busiest_resident + offsets) % experts
    return (hot_expert, busiest_resident, copies)


def destinations(chosen, replica_pick, home, hot_expert, copies, second):
    owner_dev = table_lookup(home, chosen)
    if not second:
        zeros_like = jnp.zeros_like(owner_dev)
        return (owner_dev, zeros_like, owner_dev, zeros_like)
    replica_number = replica_pick % (COPIES + 1)
    to_copy = (chosen == hot_expert) & (replica_number > 0)
    target = table_lookup(copies, replica_number - 1)
    replica_dev = jnp.where(to_copy, target, owner_dev)
    return (replica_dev, to_copy.astype(jnp.int32), owner_dev, replica_number)


def front_sums(shard_piece, groups):
    results = []
    offset = 0
    for span_count, weight_in, weight_out in groups:
        slot_block = shard_piece[:, offset : offset + span_count]
        results.append(
            jnp.einsum("nsrf,gfh->nsrgh", slot_block, weight_in, preferred_element_type=jnp.float32)
        )
        offset += span_count
    return tuple(results)


def shards(
    tokens_one,
    experts_one,
    gates_one,
    tokens_two,
    experts_two,
    gates_two,
    replica_pick,
    home,
    w_gate_up,
    w_down,
):
    devices = lax.axis_size("expert")
    tok_rows = tokens_one.shape[0]
    slot_rows = tok_rows * TOPK // devices
    assigned = tok_rows * TOPK
    indices = tally_counts(home.shape[0])
    local_counts = jnp.sum(
        (experts_one.reshape(-1)[:, None] == indices[None, :]).astype(jnp.int32),
        axis=0,
        dtype=jnp.int32,
    )
    counts = lax.psum(local_counts, "expert")
    hot_expert, busiest_resident, copies = layout_from_demand(counts, home)
    own_in = w_gate_up[0]
    own_out = w_down[0]
    moved_weights = [from_root(weight, "expert", busiest_resident) for weight in (own_in, own_out)]
    outputs = []
    batches = (
        (tokens_one, experts_one, gates_one, False),
        (tokens_two, experts_two, gates_two, True),
    )
    for tokens, chosen, gates, second in batches:
        replica_dev, replica_slot, owner_dev, replica_number = destinations(
            chosen, replica_pick, home, hot_expert, copies, second
        )
        if second:
            target_dev = replica_dev
            target_slot = replica_slot
            slot_count = 2
            groups = ((1, own_in, own_out), (1, moved_weights[0], moved_weights[1]))
        else:
            target_dev, target_slot, slot_count, groups = (
                replica_dev,
                replica_slot,
                1,
                ((1, own_in, own_out),),
            )
        slot_rank = rank_within((replica_dev * 2 + replica_slot).reshape(-1), 2 * devices)
        is_kept = slot_rank < slot_rows
        buffer_len = devices * slot_count * slot_rows
        where_to = ((target_dev * slot_count + target_slot) * slot_rows).reshape(-1) + slot_rank
        where_to = jnp.where(is_kept, where_to, buffer_len)
        source_row = (
            jnp.zeros((buffer_len + 1,), jnp.int32).at[where_to].set(tally_counts(assigned) // TOPK)
        )
        filled = jnp.zeros((buffer_len + 1,), jnp.bool_).at[where_to].set(True)
        full_rows = lax.all_gather(tokens, "inner", axis=1, tiled=True)
        outgoing = jnp.where(
            filled[:buffer_len, None],
            full_rows[source_row[:buffer_len]],
            jnp.zeros((), jnp.bfloat16),
        )
        outgoing = outgoing.reshape(devices, slot_count * slot_rows, full_rows.shape[1])
        arrived = lax.all_to_all(outgoing, "expert", split_axis=0, concat_axis=0, tiled=True)
        arrived = arrived.reshape(devices, slot_count, slot_rows, full_rows.shape[1])
        sums = front_sums(arrived, groups)
        actives = [
            (jax.nn.silu(summed_part[..., 0, :]) * summed_part[..., 1, :]).astype(jnp.bfloat16)
            for summed_part in sums
        ]
        down_parts = []
        for active, group in zip(actives, groups):
            down_parts.append(
                jnp.einsum("nsrh,hd->nsrd", active, group[2], preferred_element_type=jnp.float32)
            )
        partial_value = jnp.concatenate(down_parts, axis=1)
        summed = lax.psum_scatter(partial_value, "inner", scatter_dimension=3, tiled=True).astype(
            jnp.bfloat16
        )
        returned = lax.all_to_all(
            summed.reshape(devices, slot_count * slot_rows, summed.shape[3]),
            "expert",
            split_axis=0,
            concat_axis=0,
            tiled=True,
        )
        flat_rows = returned.reshape(buffer_len, summed.shape[3])
        flat_rows = jnp.concatenate(
            [flat_rows, jnp.zeros((1, summed.shape[3]), jnp.bfloat16)], axis=0
        )
        picked = flat_rows[where_to].astype(jnp.float32)
        weighted = gates.reshape(-1)[:, None] * picked
        outputs.append(jnp.sum(weighted.reshape(tok_rows, TOPK, -1), axis=1).astype(jnp.bfloat16))
    return (outputs[0], outputs[1])


def solution(mesh):
    placed = (
        P("expert", "inner"),
        P("expert", None),
        P("expert", None),
        P("expert", "inner"),
        P("expert", None),
        P("expert", None),
        P("expert", None),
        P(),
        P("expert", None, None, "inner"),
        P("expert", "inner", None),
    )
    return jax.shard_map(
        shards,
        mesh=mesh,
        in_specs=placed,
        out_specs=(P("expert", "inner"), P("expert", "inner")),
        check_vma=False,
    )
```

profile of v0, /device:TPU:1, one launch (start us, length us, event | category | flops | bytes accessed | tf_op | source)
XLA Modules:
  0.0 522.7 jit_solution(4928797756084054622)
XLA Ops:
  8.0 0.8 copy.75
  8.8 0.8 copy.83
  9.5 1.3 select_reduce_fusion.1
  11.0 0.1 mul.100
  11.1 0.1 mul.98
  11.2 11.0 %all_gather.6 = bf16[16,7168]{1,0:T(8,128)(2,1)S(1)} all-gather(bf16[16,1792]{1,0:T(8,128)(2,1)} %param.10), channel_id=1, replica_groups=mesh['expert'=64,'inner'=4] {'inner'}, dimensions={1}, use_global_device_ids=true | all-gather | bytes 286720 | tf_op jit(solution)/shard_map/all_gather | solution.py:121
  22.2 0.1 fusion.34
  22.3 0.2 reduce_window_sum.17
  22.5 0.2 select_reduce_fusion.2
  22.7 1.0 scatter_custom_fusion.1
  23.7 1.7 gather_fusion
  25.4 1.6 gather.17
  27.1 1.0 scatter_custom_fusion
  28.1 0.1 broadcast_in_dim.105
  28.2 4.4 broadcast_select_fusion.1
  32.6 14.9 %all-to-all-start = ((bf16[64,2,7168]{2,1,0:T(2,128)(2,1)}), bf16[64,2,7168]{2,1,0:T(2,128)(2,1)S(1)}, u32[]{:S(2)}, u32[]{:S(2)}) async-start(bf16[64,2,7168]{2,1,0:T(2,128)(2,1)} %broadcast_select_fusion.1), calls=%async_computation | async-start | bytes 3670016 | tf_op jit(solution)/shard_map/all_to_all | solution.py:128
  47.5 0.1 eq.113
  47.6 0.1 convert_reduce_fusion
  47.7 47.5 %psum.21 = s32[64]{0:T(128)S(1)} all-reduce(s32[64]{0:T(128)S(1)} %convert_reduce_fusion), channel_id=1, replica_groups=mesh['expert'=64,'inner'=4] {'expert'}, use_global_device_ids=true, to_apply=%region_8.9 | all-reduce | flops 64 | bytes 512 | tf_op jit(solution)/shard_map/psum | solution.py:86
  95.2 0.7 iota_reduce_fusion
  95.9 1.3 fusion.43
  97.8 6.7 %bitcast_select_fusion = bf16[2,7168,256]{2,1,0:T(8,128)(2,1)} fusion(bf16[1,2,7168,256]{3,2,1,0:T(8,128)(2,1)} %param.18, pred[]{:T(512)S(6)} %eq.131), kind=kLoop, calls=%fused_computation.18 | loop fusion | flops 3670016 | bytes 14680065 | tf_op jit(solution)/shard_map/jit(_where)/select_n | solution.py:11
  104.5 2.1 bitcast_select_fusion.1
  106.7 0.7 and_select_fusion
  107.4 0.1 select_reduce_fusion.4
  107.5 0.7 broadcast_multiply_fusion
  108.2 0.1 reshape.214
  108.4 0.1 eq.127
  108.5 0.1 fusion.31
  108.6 0.2 reduce_window_sum.18
  108.7 0.2 select_reduce_fusion
  108.9 1.0 scatter_custom_fusion.3
  109.9 1.0 scatter_custom_fusion.2
  110.9 9.5 %all_gather.7 = bf16[16,7168]{1,0:T(8,128)(2,1)S(1)} all-gather(bf16[16,1792]{1,0:T(8,128)(2,1)S(1)} %copy-done.6), channel_id=1, replica_groups=mesh['expert'=64,'inner'=4] {'inner'}, dimensions={1}, use_global_device_ids=true | all-gather | bytes 286720 | tf_op jit(solution)/shard_map/all_gather | solution.py:121
  120.4 4.7 gather_fusion.2
  125.2 7.0 %gather.20 = bf16[64,4,7168]{2,1,0:T(4,128)(2,1)} reshape(bf16[256,7168]{1,0:T(8,128)(2,1)} %gather_fusion.2) | data formatting | bytes 7340032 | tf_op jit(solution)/shard_map/gather | solution.py:124
  132.2 0.1 broadcast_in_dim.115
  132.3 5.4 %broadcast_select_fusion = bf16[64,4,7168]{2,1,0:T(4,128)(2,1)} fusion(bf16[64,4,7168]{2,1,0:T(4,128)(2,1)} %gather.20, pred[64,4]{1,0:T(8,128)(4,1)S(1)} %broadcast_in_dim.115), kind=kLoop, calls=%fused_computation.23 | loop fusion | flops 1835008 | bytes 7340288 | tf_op jit(solution)/shard_map/jit(_where)/select_n | solution.py:122
  137.8 13.6 %all-to-all-start.2 = ((bf16[64,4,7168]{2,1,0:T(4,128)(2,1)}), bf16[64,4,7168]{2,1,0:T(4,128)(2,1)}, u32[]{:S(2)}, u32[]{:S(2)}) async-start(bf16[64,4,7168]{2,1,0:T(4,128)(2,1)} %broadcast_select_fusion), calls=%async_computation.3 | async-start | bytes 7340032 | tf_op jit(solution)/shard_map/all_to_all | solution.py:128
  151.4 4.6 fusion.10
  156.0 2.5 convolution_bitcast_fusion.2
  158.6 0.3 reduce-scatter.5.cloned.1.call-start
  158.9 89.2 %all-to-all-done.2 = bf16[64,4,7168]{2,1,0:T(4,128)(2,1)} async-done(((bf16[64,4,7168]{2,1,0:T(4,128)(2,1)}), bf16[64,4,7168]{2,1,0:T(4,128)(2,1)}, u32[]{:S(2)}, u32[]{:S(2)}) %all-to-all-start.2) | async-done | bytes 3670048 | tf_op jit(solution)/shard_map/all_to_all | solution.py:128
  248.1 3.1 copy.87
  251.2 5.6 %fusion.15 = f32[64,1,2,2,256]{4,0,3,2,1:T(8,128)S(1)} fusion(bf16[1,2,7168,256]{3,2,1,0:T(8,128)(2,1)} %param.18, bf16[64,2,2,7168]{3,0,2,1:T(8,128)(2,1)S(1)} %bitcast.105), kind=kOutput, calls=%fused_computation.29 | convolution fusion | flops 939524096 | bytes 9437184 | tf_op jit(solution)/shard_map/nsrf,gfh->nsrgh/dot_general | solution.py:58
  256.9 2.5 convolution_bitcast_fusion.1
  259.4 127.9 %all-reduce.5.cloned.1.call-done = (bf16[256,7168]{1,0:T(8,128)(2,1)}, bf16[2,7168,256]{2,1,0:T(8,128)(2,1)}) async-done(((bf16[256,7168]{1,0:T(8,128)(2,1)}, bf16[2,7168,256]{2,1,0:T(8,128)(2,1)}), (bf16[256,7168]{1,0:T(8,128)(2,1)}, bf16[2,7168,256]{2,1,0:T(8,128)(2,1)})) %all-reduce.5.cloned.1.call-update) | async-done | bytes 11010064 | tf_op jit(solution)/shard_map/psum | solution.py:12
  387.3 4.9 fusion.18
  392.2 0.7 convolution_bitcast_fusion
  392.9 1.4 copy-done.3
  394.2 3.8 pad_maximum_fusion
  398.1 1.2 convert_bitcast_fusion
  399.3 1.3 copy.80
  400.6 9.7 %all-to-all-start.1 = ((bf16[64,2,1792]{2,1,0:T(2,128)(2,1)}), bf16[64,2,1792]{2,1,0:T(2,128)(2,1)S(1)}, u32[]{:S(2)}, u32[]{:S(2)}) async-start(bf16[64,2,1792]{2,1,0:T(2,128)(2,1)} %copy.80), calls=%async_computation.2 | async-start | bytes 917504 | tf_op jit(solution)/shard_map/all_to_all | solution.py:144
  410.2 63.0 %reduce-scatter.5.cloned.1.call-done = f32[64,2,2,1792]{3,0,2,1:T(8,128)} async-done(((f32[64,2,2,7168]{3,0,2,1:T(8,128)}), f32[64,2,2,1792]{3,0,2,1:T(8,128)}) %reduce-scatter.5.cloned.1.call-update) | async-done | bytes 1835024 | tf_op jit(solution)/shard_map/reduce_scatter | solution.py:141
  473.3 1.6 convert_element_type.79
  474.9 1.6 copy.89
  476.5 10.7 %all-to-all-start.3 = ((bf16[64,4,1792]{2,1,0:T(4,128)(2,1)}), bf16[64,4,1792]{2,1,0:T(4,128)(2,1)S(1)}, u32[]{:S(2)}, u32[]{:S(2)}) async-start(bf16[64,4,1792]{2,1,0:T(4,128)(2,1)} %copy.89), calls=%async_computation.5 | async-start | bytes 1835008 | tf_op jit(solution)/shard_map/all_to_all | solution.py:144
  487.4 0.2 reshape.213
  487.6 0.9 gather_fusion.1
  488.5 24.0 %all-to-all-done.3 = bf16[64,4,1792]{2,1,0:T(4,128)(2,1)S(1)} async-done(((bf16[64,4,1792]{2,1,0:T(4,128)(2,1)}), bf16[64,4,1792]{2,1,0:T(4,128)(2,1)S(1)}, u32[]{:S(2)}, u32[]{:S(2)}) %all-to-all-start.3) | async-done | bytes 917536 | tf_op jit(solution)/shard_map/all_to_all | solution.py:144
  512.5 0.2 reshape.219
  512.8 0.9 gather_fusion.3
  513.7 1.6 fusion.21
  (52 shorter events, 0.9 us)
Async XLA Ops:
  28.2 67.6 %copy-start.11 = (s32[64]{0:T(128)S(1)}, s32[64]{0:T(128)}, u32[]{:S(2)}) copy-start(s32[64]{0:T(128)} %param.17) | copy-start | bytes 772
  32.6 105.2 %all-to-all-start = ((bf16[64,2,7168]{2,1,0:T(2,128)(2,1)}), bf16[64,2,7168]{2,1,0:T(2,128)(2,1)S(1)}, u32[]{:S(2)}, u32[]{:S(2)}) async-start(bf16[64,2,7168]{2,1,0:T(2,128)(2,1)} %broadcast_select_fusion.1), calls=%async_computation | async-start | bytes 3670016 | tf_op jit(solution)/shard_map/all_to_all | solution.py:128
  47.5 339.8 %all-reduce.5.cloned.1.call-start = ((), (), s32[]{:S(2)}) async-start(), calls=%async_computation.8 | async-start | bytes 22020096 | tf_op jit(solution)/shard_map/psum | solution.py:12
  97.8 6.7 %copy-start = (bf16[1,256,7168]{2,1,0:T(8,128)(2,1)S(1)}, bf16[1,256,7168]{2,1,0:T(8,128)(2,1)}, u32[]{:S(2)}) copy-start(bf16[1,256,7168]{2,1,0:T(8,128)(2,1)} %param.19) | copy-start | bytes 11010052
  106.6 0.8 copy-start.8
  106.6 0.9 copy-start.7
  106.6 4.3 copy-start.6
  137.8 110.3 %all-to-all-start.2 = ((bf16[64,4,7168]{2,1,0:T(4,128)(2,1)}), bf16[64,4,7168]{2,1,0:T(4,128)(2,1)}, u32[]{:S(2)}, u32[]{:S(2)}) async-start(bf16[64,4,7168]{2,1,0:T(4,128)(2,1)} %broadcast_select_fusion), calls=%async_computation.3 | async-start | bytes 7340032 | tf_op jit(solution)/shard_map/all_to_all | solution.py:128
  151.4 246.7 %reduce-scatter.3.cloned.1.call-start = ((), (), s32[]{:S(2)}) async-start(), calls=%async_computation.6 | async-start | bytes 4587520 | tf_op jit(solution)/shard_map/reduce_scatter | solution.py:141
  151.4 4.6 copy-start.1
  158.6 314.7 %reduce-scatter.5.cloned.1.call-start = ((), (), s32[]{:S(2)}) async-start(), calls=%async_computation.7 | async-start | bytes 9175040 | tf_op jit(solution)/shard_map/reduce_scatter | solution.py:141
  251.2 5.7 %copy-start.5 = (bf16[64,4,7168]{2,0,1:T(8,128)(2,1)}, bf16[64,4,7168]{2,0,1:T(8,128)(2,1)S(1)}, u32[]{:S(2)}) copy-start(bf16[64,4,7168]{2,0,1:T(8,128)(2,1)S(1)} %copy.87) | copy-start | bytes 11010052
  251.2 5.7 %copy-start.2 = (bf16[1,256,7168]{2,1,0:T(8,128)(2,1)S(1)}, bf16[1,256,7168]{2,1,0:T(8,128)(2,1)}, u32[]{:S(2)}) copy-start(bf16[1,256,7168]{2,1,0:T(8,128)(2,1)} %param.19) | copy-start | bytes 11010052
  387.3 4.9 copy-start.4
  392.2 2.0 copy-start.3
  400.6 86.7 %copy-start.9 = (f32[16,8]{0,1:T(8,128)S(1)}, f32[16,8]{0,1:T(8,128)}, u32[]{:S(2)}) copy-start(f32[16,8]{0,1:T(8,128)} %param.15) | copy-start | bytes 1540
  400.6 86.7 %copy-start.10 = (f32[16,8]{0,1:T(8,128)S(1)}, f32[16,8]{0,1:T(8,128)}, u32[]{:S(2)}) copy-start(f32[16,8]{0,1:T(8,128)} %param.12) | copy-start | bytes 1540
  400.6 75.9 %all-to-all-start.1 = ((bf16[64,2,1792]{2,1,0:T(2,128)(2,1)}), bf16[64,2,1792]{2,1,0:T(2,128)(2,1)S(1)}, u32[]{:S(2)}, u32[]{:S(2)}) async-start(bf16[64,2,1792]{2,1,0:T(2,128)(2,1)} %copy.80), calls=%async_computation.2 | async-start | bytes 917504 | tf_op jit(solution)/shard_map/all_to_all | solution.py:144
  476.5 36.0 %all-to-all-start.3 = ((bf16[64,4,1792]{2,1,0:T(4,128)(2,1)}), bf16[64,4,1792]{2,1,0:T(4,128)(2,1)S(1)}, u32[]{:S(2)}, u32[]{:S(2)}) async-start(bf16[64,4,1792]{2,1,0:T(4,128)(2,1)} %copy.89), calls=%async_computation.5 | async-start | bytes 1835008 | tf_op jit(solution)/shard_map/all_to_all | solution.py:144
Sparse Core Ops, SparseCore 0:
  106.8 280.4 all-reduce.4
Sparse Core Ops, SparseCore 1:
  158.7 45.2 reduce-scatter.2
  398.1 75.1 reduce-scatter.4
where the time goes:
time: 524 us; the launch traced here: 523 us
  waiting for transfers between devices  304 us (58%)
  blocking collectives  68 us (13%)
  starting transfers between devices  49.2 us (9%)
  other arithmetic  32.5 us (6%)
  local copies, waits for them, and re-layouts  31.6 us (6%)
  matrix products  20.8 us (4%)
  between operations  16.5 us (3%)
    psum x1, waiting for transfers between devices, from_root(): return lax.psum(kept, axis)  128 us
    all_to_all x2, waiting for transfers between devices, shards(): lax.all_to_all(outgoing, 'expert', split_axis=0, concat_axis=0, tiled=True)  89.2 us
    reduce_scatter x2, waiting for transfers between devices, shards(): lax.psum_scatter(partial_value, 'inner', scatter_dimension=3, tiled=True)  63.1 us
    psum x1, blocking collectives, shards(): counts = lax.psum(local_counts, 'expert')  47.5 us
    all_to_all x2, starting transfers between devices, shards(): lax.all_to_all(outgoing, 'expert', split_axis=0, concat_axis=0, tiled=True)  28.5 us
    all_to_all x2, waiting for transfers between devices, shards(): lax.all_to_all(summed.reshape(devices, slot_count * slot_rows, summed.sha...  24 us
    all_gather x2, blocking collectives, shards(): full_rows = lax.all_gather(tokens, 'inner', axis=1, tiled=True)  20.5 us
    all_to_all x2, starting transfers between devices, shards(): lax.all_to_all(summed.reshape(devices, slot_count * slot_rows, summed.sha...  20.4 us
  transfers between devices with their start and end apart: 7, of which 4 were waited for; matrix products, arithmetic and copies ran while one was open for 13% of the time, Pallas kernels for 0%

commit v1 on v0

v1 whole, which is shorter than its diff:
```python
import functools

import jax
import jax.numpy as jnp
from jax import lax
from jax.experimental import pallas as pl
from jax.experimental.pallas import tpu as pltpu
from jax.sharding import PartitionSpec as P

MESH = pl.DeviceIdType.MESH
TOPK = 8
COPIES = 3
SLOT = 2
CORES = 2
F32 = jnp.float32
BF16 = jnp.bfloat16
E1, G1, E2, G2, PICK = 0, 8, 16, 24, 32


def dot(a, b):
    return jnp.dot(a, b, preferred_element_type=F32)


def iota(shape, dim):
    return lax.broadcasted_iota(jnp.int32, shape, dim)


class Copies:
    def __init__(self, n, me, src, dst, device, send, recv):
        self.items = []
        for i in range(1, n):
            peer = lax.rem(me + i, n)
            self.items.append(
                pltpu.make_async_remote_copy(
                    src_ref=src(peer),
                    dst_ref=dst(me),
                    send_sem=send.at[i],
                    recv_sem=recv.at[i],
                    device_id=device(peer),
                    device_id_type=MESH,
                )
            )

    def start(self):
        for item in self.items:
            item.start()

    def wait_recv(self):
        for item in self.items:
            item.wait_recv()

    def wait_send(self):
        for item in self.items:
            item.wait_send()


class Ring:
    def __init__(self, n, me, block, half, device, send, recv):
        self.steps = n // 2
        self.pairs = []
        right, left = lax.rem(me + 1, n), lax.rem(me + n - 1, n)
        for k in range(1, self.steps + 1):
            pair = []
            for way, (target, index) in enumerate(
                ((right, lax.rem(me + n - (k - 1), n)), (left, lax.rem(me + (k - 1), n)))
            ):
                ref = half(index, way) if k == self.steps else block(index)
                pair.append(
                    pltpu.make_async_remote_copy(
                        src_ref=ref,
                        dst_ref=ref,
                        send_sem=send.at[2 * k + way],
                        recv_sem=recv.at[2 * k + way],
                        device_id=device(target),
                        device_id_type=MESH,
                    )
                )
            self.pairs.append(pair)

    def start(self, k):
        for item in self.pairs[k - 1]:
            item.start()

    def wait_recv(self, k):
        for item in self.pairs[k - 1]:
            item.wait_recv()

    def wait_send(self):
        for pair in self.pairs:
            for item in pair:
                item.wait_send()


def kernel(
    dims,
    tok1,
    tok2,
    info_in,
    home,
    w_in,
    w_out,
    out1,
    out2,
    z1,
    z2,
    info,
    counts,
    xs1,
    y1,
    xs2,
    xr2,
    hid1,
    hid2,
    wgu,
    wd,
    acc,
    o1,
    o2,
    ro1,
    ro2,
    mix1,
    mix2,
    mr1,
    mr2,
    local,
    *sems,
):
    nz, nx, ny = dims
    npl = nx * CORES
    tok = tok1.shape[0]
    feat = tok1.shape[1]
    width = feat * ny
    ff = w_in.shape[3]
    cols = nz * tok
    s1 = SLOT * nz
    s2 = (COPIES + 1) * s1
    sems = list(sems)

    e = lax.axis_index("expert")
    y = lax.axis_index("inner")
    z = e // npl
    p = lax.rem(e, npl)
    x = p // CORES
    c = lax.rem(p, CORES)
    zdev = lambda other: (other * npl + p, y)
    pdev = lambda other: (z * npl + other, y)
    ydev = lambda other: (e, other)
    xdev = lambda other: (z * npl + other * CORES + c, y)

    def pair():
        return sems.pop(0), sems.pop(0)

    def rows(ref, start, size):
        return ref.at[pl.ds(start, size)]

    def lanes(ref, index, size):
        return ref.at[:, pl.ds(pl.multiple_of(index * size, size), size)]

    def block(ref, r, rs, l, ls):
        return ref.at[pl.ds(r, rs), pl.ds(pl.multiple_of(l, ls), ls)]

    weights = pltpu.make_async_copy(w_in.at[0], wgu, local.at[0])
    weights.start()
    own_out = pltpu.make_async_copy(
        lanes(w_out.at[0], y, feat), rows(wd, y * ff, ff), local.at[1]
    )
    own_out.start()

    barrier = pltpu.get_barrier_semaphore()
    for i in range(1, nz):
        pl.semaphore_signal(barrier, inc=1, device_id=zdev(lax.rem(z + i, nz)), device_id_type=MESH)
    for i in range(1, npl):
        pl.semaphore_signal(barrier, inc=1, device_id=pdev(lax.rem(p + i, npl)), device_id_type=MESH)
    for i in range(1, ny):
        pl.semaphore_signal(barrier, inc=1, device_id=ydev(lax.rem(y + i, ny)), device_id_type=MESH)
    pl.semaphore_wait(barrier, nz + npl + ny - 3)

    started = []

    def go(copies):
        copies.start()
        started.append(copies)
        return copies

    info_z = go(Copies(nz, z, lambda o: info_in, lambda m: rows(info, m * tok, tok), zdev, *pair()))
    tok2_y = go(Copies(ny, y, lambda o: tok2, lambda m: lanes(rows(z2, z * tok, tok), m, feat), ydev, *pair()))
    tok1_z = go(Copies(nz, z, lambda o: tok1, lambda m: rows(z1, m * tok, tok), zdev, *pair()))
    info[pl.ds(z * tok, tok), :] = info_in[...]
    z1[pl.ds(z * tok, tok), :] = tok1[...]
    z2[pl.ds(z * tok, tok), pl.ds(pl.multiple_of(y * feat, feat), feat)] = tok2[...]
    tok2_y.wait_recv()
    ring2 = Ring(
        nz,
        z,
        lambda i: rows(z2, i * tok, tok),
        lambda i, h: block(z2, i * tok, tok, h * (width // 2), width // 2),
        zdev,
        *pair(),
    )
    ring2.start(1)
    out_y = go(
        Copies(
            ny, y, lambda o: lanes(w_out.at[0], o, feat), lambda m: rows(wd, m * ff, ff), ydev, *pair()
        )
    )

    info_z.wait_recv()
    every = info[...]
    turned = every.T
    field = lambda base, k: turned[base + k : base + k + 1, :]
    expert_lane = iota((cols, 128), 1).astype(F32)
    tally = jnp.zeros((cols, 128), F32)
    for k in range(TOPK):
        tally += (every[:, E1 + k : E1 + k + 1] == expert_lane).astype(F32)
    own_counts = jnp.broadcast_to(jnp.sum(tally, axis=0, keepdims=True), (8, 128))
    counts[pl.ds(p * 8, 8), :] = own_counts
    counts_p = go(
        Copies(npl, p, lambda o: rows(counts, p * 8, 8), lambda m: rows(counts, m * 8, 8), pdev, *pair())
    )

    shape = (cols, cols)
    earlier = ((iota(shape, 0) // tok == iota(shape, 1) // tok) & (iota(shape, 0) < iota(shape, 1))).astype(BF16)

    def resident(length, per):
        target = z * npl + iota((length, 128), 0) // per
        holds = home[0:1, :] == target
        lane = iota((length, 128), 1).astype(F32)
        return jnp.sum(jnp.where(holds, lane, 0.0), axis=1, keepdims=True)

    def selection(match, length):
        number = dot(match.astype(BF16), earlier)
        slot = (iota((length, cols), 0) // nz % SLOT).astype(F32)
        return jnp.where(number == slot, match, 0.0)

    n1 = npl * s1
    same_z = (iota((n1, cols), 0) % nz) == (iota((n1, cols), 1) // tok)
    holder = resident(n1, s1)
    match = jnp.zeros((n1, cols), F32)
    gate = jnp.zeros((n1, cols), F32)
    for k in range(TOPK):
        hit = (field(E1, k) == holder) & same_z
        match += hit.astype(F32)
        gate += jnp.where(hit, field(G1, k), 0.0)
    sel1 = selection(match, n1)
    mixer1 = (sel1 * gate).T

    tok1_z.wait_recv()
    xs1[...] = dot(sel1.astype(BF16), z1[...]).astype(BF16)
    mine = lambda ref: lanes(ref, y, feat)
    x1 = go(
        Copies(
            npl, p, lambda o: rows(xs1, o * s1, s1), lambda m: mine(rows(y1, m * s1, s1)), pdev, *pair()
        )
    )
    y1[pl.ds(p * s1, s1), pl.ds(pl.multiple_of(y * feat, feat), feat)] = xs1[pl.ds(p * s1, s1), :]

    counts_p.wait_recv()
    total = counts[0:8, :]
    for other in range(1, npl):
        total += counts[other * 8 : other * 8 + 8, :]
    total = total[0:1, :]
    lane = iota((1, 128), 1)
    experts = nz * npl
    total = jnp.where(lane < experts, total, -1.0)
    most = jnp.max(total, axis=1, keepdims=True)
    hot = jnp.min(jnp.where(total == most, lane.astype(F32), 1e6), axis=1, keepdims=True)

    n2 = npl * s2
    same_z = (iota((n2, cols), 0) % nz) == (iota((n2, cols), 1) // tok)
    holder = resident(n2, s2)
    copy_number = (iota((n2, cols), 0) // s1 % (COPIES + 1)).astype(F32)
    match = jnp.zeros((n2, cols), F32)
    gate = jnp.zeros((n2, cols), F32)
    for k in range(TOPK):
        chosen, pick = field(E2, k), field(PICK, k)
        number = jnp.where(chosen == hot, pick, 0.0)
        wanted = jnp.where(copy_number > 0.0, hot, holder)
        hit = (chosen == wanted) & (number == copy_number) & same_z
        match += hit.astype(F32)
        gate += jnp.where(hit, field(G2, k), 0.0)
    sel2 = selection(match, n2)
    here = jnp.where((copy_number == 0.0) | (holder == hot), sel2 * gate, 0.0)
    mixer2 = here.T
    sel2 = sel2.astype(BF16)

    for k in range(2, ring2.steps + 1):
        ring2.wait_recv(k - 1)
        ring2.start(k)

    x1.wait_recv()
    y1_y = go(Copies(ny, y, lambda o: mine(y1), lambda m: lanes(y1, m, feat), ydev, *pair()))

    ring2.wait_recv(ring2.steps)
    regular = jnp.concatenate([sel2[i * s2 : i * s2 + s1] for i in range(npl)], axis=0)
    extra = sel2[s1:s2]
    hot_rows = s2 - s1
    pieces = 2 * ny
    step = width // pieces
    for i in range(pieces):
        columns = slice(i * step, (i + 1) * step)
        xr2[pl.ds(p * s2 + s1, hot_rows), columns] = dot(extra, z2[:, columns]).astype(BF16)
    hot_block = lambda o: rows(xr2, o * s2 + s1, hot_rows)
    xc = lambda o: o * CORES + c
    ringh = Ring(
        nx,
        x,
        lambda i: hot_block(xc(i)),
        lambda i, h: block(xr2, xc(i) * s2 + s1, hot_rows, h * (width // 2), width // 2),
        xdev,
        *pair(),
    )
    ringh.start(1)
    for i in range(pieces):
        columns = slice(i * step, (i + 1) * step)
        xs2[:, columns] = dot(regular, z2[:, columns]).astype(BF16)
    x2 = go(Copies(npl, p, lambda o: rows(xs2, o * s1, s1), lambda m: rows(xr2, m * s2, s1), pdev, *pair()))
    xr2[pl.ds(p * s2, s1), :] = xs2[pl.ds(p * s1, s1), :]
    sib_send, sib_recv = pair()
    sibling = []

    def to_sibling(i):
        item = pltpu.make_async_remote_copy(
            src_ref=hot_block(xc(i)),
            dst_ref=hot_block(xc(i)),
            send_sem=sib_send.at[len(sibling)],
            recv_sem=sib_recv.at[len(sibling)],
            device_id=pdev(x * CORES + 1 - c),
            device_id_type=MESH,
        )
        item.start()
        sibling.append(item)

    to_sibling(x)

    def front(lhs, length):
        acc[pl.ds(0, length), :] = jnp.zeros((length, 2 * ff), F32)

        @pl.loop(0, ny)
        def _(q):
            part = pl.ds(pl.multiple_of(q * feat, feat), feat)
            a = lhs[:, part]
            for i in range(2):
                acc[pl.ds(0, length), i * ff : (i + 1) * ff] += dot(a, wgu[i, part, :])

    def active(hid, length):
        gated = acc[pl.ds(0, length), 0:ff]
        value = gated / (1.0 + jnp.exp(-gated)) * acc[pl.ds(0, length), ff : 2 * ff]
        hid[:, pl.ds(pl.multiple_of(y * ff, ff), ff)] = value.astype(BF16)

    def gather_hidden(hid):
        return go(Copies(ny, y, lambda o: lanes(hid, y, ff), lambda m: lanes(hid, m, ff), ydev, *pair()))

    weights.wait()
    y1_y.wait_recv()
    front(y1, n1)
    active(hid1, n1)
    hid1_y = gather_hidden(hid1)

    for k in range(1, ringh.steps + 1):
        ringh.wait_recv(k)
        if k < ringh.steps:
            ringh.start(k + 1)
            to_sibling(lax.rem(x + nx - k, nx))
            to_sibling(lax.rem(x + k, nx))
        else:
            to_sibling(lax.rem(x + k, nx))

    own_out.wait()
    out_y.wait_recv()
    hid1_y.wait_recv()
    o1[...] = dot(hid1[...], wd[...]).astype(BF16)
    r1 = go(
        Copies(npl, p, lambda o: rows(o1, o * s1, s1), lambda m: rows(ro1, m * s1, s1), pdev, *pair())
    )
    ro1[pl.ds(p * s1, s1), :] = o1[pl.ds(p * s1, s1), :]

    x2.wait_recv()
    for item in sibling:
        item.wait_recv()
    front(xr2, n2)
    active(hid2, n2)
    hid2_y = gather_hidden(hid2)

    def mix(mixer, ro, out, inbox):
        high = mixer.astype(BF16)
        low = (mixer - high.astype(F32)).astype(BF16)
        out[...] = (dot(high, ro[...]) + dot(low, ro[...])).astype(BF16)
        copies = go(
            Copies(nz, z, lambda o: rows(out, o * tok, tok), lambda m: rows(inbox, m * tok, tok), zdev, *pair())
        )
        inbox[pl.ds(z * tok, tok), :] = out[pl.ds(z * tok, tok), :]
        return copies

    r1.wait_recv()
    m1 = mix(mixer1, ro1, mix1, mr1)

    hid2_y.wait_recv()

    tile = min(n2, 128)

    @pl.loop(0, n2 // tile)
    def _(i):
        part = pl.ds(pl.multiple_of(i * tile, tile), tile)
        o2[part, :] = dot(hid2[part, :], wd[...]).astype(BF16)

    r2 = go(
        Copies(npl, p, lambda o: rows(o2, o * s2, s2), lambda m: rows(ro2, m * s2, s2), pdev, *pair())
    )
    ro2[pl.ds(p * s2, s2), :] = o2[pl.ds(p * s2, s2), :]

    def final(inbox, out):
        total = inbox[0:tok, :].astype(F32)
        for i in range(1, nz):
            total += inbox[i * tok : (i + 1) * tok, :].astype(F32)
        out[...] = total.astype(BF16)

    m1.wait_recv()
    final(mr1, out1)
    r2.wait_recv()
    m2 = mix(mixer2, ro2, mix2, mr2)
    m2.wait_recv()
    final(mr2, out2)

    for copies in started:
        copies.wait_send()
    ring2.wait_send()
    ringh.wait_send()
    for item in sibling:
        item.wait_send()


def shards(
    dims, tokens_one, experts_one, gates_one, tokens_two, experts_two, gates_two, replica_pick, home, w_gate_up, w_down
):
    nz, nx, ny = dims
    npl = nx * CORES
    tok, feat = tokens_one.shape
    width = feat * ny
    ff = w_gate_up.shape[3]
    info = jnp.concatenate(
        [
            experts_one.astype(F32),
            gates_one,
            experts_two.astype(F32),
            gates_two,
            (replica_pick % (COPIES + 1)).astype(F32),
            jnp.zeros((tok, 128 - 5 * TOPK), F32),
        ],
        axis=1,
    )
    home = jnp.pad(home[None, :], ((0, 7), (0, 128 - home.shape[0])), constant_values=-1)
    cols = nz * tok
    n1 = npl * SLOT * nz
    n2 = n1 * (COPIES + 1)
    vmem = pltpu.VMEM
    dma = pltpu.SemaphoreType.DMA
    groups = [nz, ny, nz, nz + 2, ny, npl, npl, ny, nx + 2, npl, nx, ny, npl, ny, nz, npl, nz]
    any_spec = pl.BlockSpec(memory_space=pl.ANY)
    in_vmem = pl.BlockSpec(memory_space=pltpu.VMEM)
    return pl.pallas_call(
        functools.partial(kernel, dims),
        out_shape=[jax.ShapeDtypeStruct((tok, feat), BF16)] * 2,
        in_specs=[in_vmem] * 4 + [any_spec] * 2,
        out_specs=[in_vmem] * 2,
        scratch_shapes=[
            vmem((cols, feat), BF16),
            vmem((cols, width), BF16),
            vmem((cols, 128), F32),
            vmem((npl * 8, 128), F32),
            vmem((n1, feat), BF16),
            vmem((n1, width), BF16),
            vmem((n1, width), BF16),
            vmem((n2, width), BF16),
            vmem((n1, ff * ny), BF16),
            vmem((n2, ff * ny), BF16),
            vmem(w_gate_up.shape[1:], BF16),
            vmem((ff * ny, feat), BF16),
            vmem((n2, 2 * ff), F32),
            vmem((n1, feat), BF16),
            vmem((n2, feat), BF16),
            vmem((n1, feat), BF16),
            vmem((n2, feat), BF16),
            vmem((cols, feat), BF16),
            vmem((cols, feat), BF16),
            vmem((cols, feat), BF16),
            vmem((cols, feat), BF16),
            dma((2,)),
        ]
        + [dma((n + 2,)) for n in groups for _ in range(2)],
        compiler_params=pltpu.CompilerParams(
            collective_id=0, has_side_effects=True, vmem_limit_bytes=56 * 1024 * 1024
        ),
        cost_estimate=pl.CostEstimate(flops=10_000_000_000, bytes_accessed=16_000_000, transcendentals=0),
    )(tokens_one, tokens_two, info, home, w_gate_up, w_down)


def solution(mesh):
    placed = (
        P("expert", "inner"),
        P("expert", None),
        P("expert", None),
        P("expert", "inner"),
        P("expert", None),
        P("expert", None),
        P("expert", None),
        P(),
        P("expert", None, None, "inner"),
        P("expert", "inner", None),
    )
    experts, inner = mesh.shape["expert"], mesh.shape["inner"]
    nx = 4 if experts >= 16 else 2
    dims = (experts // (nx * CORES), nx, inner)
    return jax.shard_map(
        functools.partial(shards, dims),
        mesh=mesh,
        in_specs=placed,
        out_specs=(P("expert", "inner"), P("expert", "inner")),
        check_vma=False,
    )
```

time: 524 us -> 158 us (0.30)
  waiting for transfers between devices: 304 us -> 0 us
  Pallas kernels: 0 us -> 149 us
  blocking collectives: 68 us -> 0 us
  starting transfers between devices: 49.2 us -> 0 us
  other arithmetic: 32.5 us -> 1.39 us
  local copies, waits for them, and re-layouts: 31.6 us -> 7.24 us
  matrix products: 20.8 us -> 0 us
  between operations: 16.5 us -> 0.65 us
    pallas_call x0 -> x1, Pallas kernels: none -> 149 us  [shards(): pl.pallas_call(functools.partial(kernel, dims), out_shape=[jax.ShapeDtype...]
    psum x1 -> x0, waiting for transfers between devices: 128 us -> none  [from_root(): return lax.psum(kept, axis)]
    all_to_all x4 -> x0, waiting for transfers between devices: 113 us -> none  [the longest x2 89.2 us: shards(): lax.all_to_all(outgoing, 'expert', split_axis=0, concat_axis=0, tiled=True)]
    reduce_scatter x2 -> x0, waiting for transfers between devices: 63.1 us -> none  [shards(): lax.psum_scatter(partial_value, 'inner', scatter_dimension=3, tiled=True)]
    all_to_all x4 -> x0, starting transfers between devices: 48.8 us -> none  [the longest x2 28.5 us: shards(): lax.all_to_all(outgoing, 'expert', split_axis=0, concat_axis=0, tiled=True)]
    psum x1 -> x0, blocking collectives: 47.5 us -> none  [shards(): counts = lax.psum(local_counts, 'expert')]
    dot_general x6 -> x0, matrix products: 20.8 us -> none  [the longest x3 15.1 us: front_sums(): jnp.einsum('nsrf,gfh->nsrgh', slot_block, weight_in, preferred_element_ty...]
    all_gather x2 -> x0, blocking collectives: 20.5 us -> none  [shards(): full_rows = lax.all_gather(tokens, 'inner', axis=1, tiled=True)]
  transfers between devices with their start and end apart: 7 -> 0, of which waited for: 4 -> 0; matrix products, arithmetic and copies ran while one was open for 13% -> 0% of each run, Pallas kernels for 0% -> 0%
where the time goes in v1:
time: 158 us
  Pallas kernels  149 us (94%)
  local copies, waits for them, and re-layouts  7.24 us (5%)
    pallas_call x1, Pallas kernels, shards(): pl.pallas_call(functools.partial(kernel, dims), out_shape=[jax.ShapeDtype...  149 us
    unnamed x5, local copies, waits for them, and re-layouts  5.16 us

profile of v1, /device:TPU:1, one launch (start us, length us, event | category | flops | bytes accessed | tf_op | source)
XLA Modules:
  0.0 157.9 jit_solution(5468050391366800659)
XLA Ops:
  0.6 0.7 convert_element_type.9
  1.3 0.1 copy.22
  1.4 0.7 convert_element_type.10
  2.1 0.1 copy.24
  2.2 1.3 pad.4.home
  3.4 0.8 copy.23
  4.2 0.8 copy.25
  4.9 0.8 copy.19
  5.7 0.7 concatenate.3.info_in
  6.4 148.6 %shard_map.113 = (bf16[16,1792]{1,0:T(8,128)(2,1)}, bf16[16,1792]{1,0:T(8,128)(2,1)}) custom-call(bf16[16,1792]{1,0:T(8,128)(2,1)} %tok1.1, bf16[16,1792]{1,0:T(8,128)(2,1)} %tok2.1, f32[16,128]{1,0:T(8,128)} %concatenate.3.info_in, s32[8,128]{1,0:T(8,128)} %pad.4.home, bf16[1,2,7168,256]{3,2,1,0:T(8,128)(2,1)} %w_in.1, bf16[1,256,7168]{2,1,0:T(8,128)(2,1)} %w_out.1), custom_call_target="tpu_custom_call" | custom-call | flops 10000000000 | bytes 16000000 | tf_op jit(solution)/shard_map/pallas_call | solution.py:460
  155.0 1.4 copy.28
  156.4 1.4 copy.29
  (2 shorter events, 0.0 us)

commit v2 on v1

v2 whole, which is shorter than its diff:
```python
import functools

import jax
import jax.numpy as jnp
from jax import lax
from jax.experimental import pallas as pl
from jax.experimental.pallas import tpu as pltpu
from jax.sharding import PartitionSpec as P

MESH = pl.DeviceIdType.MESH
TOPK = 8
COPIES = 3
SLOT = 2
CORES = 2
F32 = jnp.float32
BF16 = jnp.bfloat16
E1, G1, E2, G2, PICK = 0, 8, 16, 24, 32


def dot(a, b):
    return jnp.dot(a, b, preferred_element_type=F32)


def iota(shape, dim):
    return lax.broadcasted_iota(jnp.int32, shape, dim)


class Copies:
    def __init__(self, n, me, src, dst, device, send, recv):
        self.items = []
        for i in range(1, n):
            peer = lax.rem(me + i, n)
            self.items.append(
                pltpu.make_async_remote_copy(
                    src_ref=src(peer),
                    dst_ref=dst(me),
                    send_sem=send.at[i],
                    recv_sem=recv.at[i],
                    device_id=device(peer),
                    device_id_type=MESH,
                )
            )

    def start(self):
        for item in self.items:
            item.start()

    def wait_from(self, ahead):
        self.items[len(self.items) - ahead].wait_recv()

    def wait_recv(self):
        for item in self.items:
            item.wait_recv()

    def wait_send(self):
        for item in self.items:
            item.wait_send()


class Ring:
    def __init__(self, n, me, block, half, device, send, recv):
        self.steps = n // 2
        self.at = 0
        self.pairs = []
        right, left = lax.rem(me + 1, n), lax.rem(me + n - 1, n)
        for k in range(1, self.steps + 1):
            pair = []
            for way, (target, index) in enumerate(
                ((right, lax.rem(me + n - (k - 1), n)), (left, lax.rem(me + (k - 1), n)))
            ):
                ref = half(index, way) if k == self.steps else block(index)
                pair.append(
                    pltpu.make_async_remote_copy(
                        src_ref=ref,
                        dst_ref=ref,
                        send_sem=send.at[2 * k + way],
                        recv_sem=recv.at[2 * k + way],
                        device_id=device(target),
                        device_id_type=MESH,
                    )
                )
            self.pairs.append(pair)

    def step(self):
        if self.at > self.steps:
            return
        if self.at > 0:
            for item in self.pairs[self.at - 1]:
                item.wait_recv()
        if self.at < self.steps:
            for item in self.pairs[self.at]:
                item.start()
        self.at += 1

    def finish(self):
        while self.at <= self.steps:
            self.step()

    def wait_send(self):
        for pair in self.pairs:
            for item in pair:
                item.wait_send()


def kernel(
    dims,
    tok1,
    tok2,
    e1,
    g1,
    e2,
    g2,
    picks,
    home,
    w_in,
    w_out,
    out,
    pack,
    info,
    counts,
    z1,
    z2,
    xs1,
    xs2,
    xr,
    acc,
    hid,
    o,
    ro,
    blend,
    mix,
    inbox,
    halves,
    wgu,
    wd,
    local,
    *sems,
):
    nz, nx, ny = dims
    npl = nx * CORES
    tok, feat = tok1.shape
    width = feat * ny
    ff = w_in.shape[3]
    cols = nz * tok
    s1 = SLOT * nz
    chunk = npl * s1
    sems = list(sems)

    e = lax.axis_index("expert")
    y = lax.axis_index("inner")
    z = e // npl
    p = lax.rem(e, npl)
    x = p // CORES
    c = lax.rem(p, CORES)
    zdev = lambda other: (other * npl + p, y)
    pdev = lambda other: (z * npl + other, y)
    ydev = lambda other: (e, other)
    xdev = lambda other: (z * npl + other * CORES + c, y)

    def pair():
        return sems.pop(0), sems.pop(0)

    def rows(ref, start, size):
        return ref.at[pl.ds(start, size)]

    def lanes(ref, index, size):
        return ref.at[:, pl.ds(pl.multiple_of(index * size, size), size)]

    def block(ref, r, rs, l, ls):
        return ref.at[pl.ds(r, rs), pl.ds(pl.multiple_of(l, ls), ls)]

    weights = pltpu.make_async_copy(w_in.at[0], wgu, local.at[0])
    weights.start()
    own_out = pltpu.make_async_copy(lanes(w_out.at[0], y, feat), rows(wd, y * ff, ff), local.at[1])
    own_out.start()

    pack[...] = jnp.zeros_like(pack)
    pack[E1 : E1 + TOPK, 0:tok] = e1[...].astype(F32)
    pack[G1 : G1 + TOPK, 0:tok] = g1[...]
    pack[E2 : E2 + TOPK, 0:tok] = e2[...].astype(F32)
    pack[G2 : G2 + TOPK, 0:tok] = g2[...]
    pack[PICK : PICK + TOPK, 0:tok] = lax.rem(picks[...], COPIES + 1).astype(F32)
    info[pl.ds(z * tok, tok), :] = pack[...].T[0:tok, :]
    z1[pl.ds(z * tok, tok), :] = tok1[...]
    z2[pl.ds(z * tok, tok), pl.ds(pl.multiple_of(y * feat, feat), feat)] = tok2[...]

    barrier = pltpu.get_barrier_semaphore()
    for i in range(1, nz):
        pl.semaphore_signal(barrier, inc=1, device_id=zdev(lax.rem(z + i, nz)), device_id_type=MESH)
    for i in range(1, npl):
        pl.semaphore_signal(barrier, inc=1, device_id=pdev(lax.rem(p + i, npl)), device_id_type=MESH)
    for i in range(1, ny):
        pl.semaphore_signal(barrier, inc=1, device_id=ydev(lax.rem(y + i, ny)), device_id_type=MESH)

    shape = (cols, cols)
    earlier = ((iota(shape, 0) // tok == iota(shape, 1) // tok) & (iota(shape, 0) < iota(shape, 1))).astype(BF16)
    here = home.shape[1]
    held = home[0:1, :] == z * npl + iota((chunk, here), 0) // s1
    holder = jnp.sum(jnp.where(held, iota((chunk, here), 1).astype(F32), 0.0), axis=1, keepdims=True)

    pl.semaphore_wait(barrier, nz + npl + ny - 3)

    started = []

    def go(copies):
        copies.start()
        started.append(copies)
        return copies

    order = [0, 1, 3, 2] if ny == 4 else list(range(ny))
    quarters = [lax.rem(y + s, ny) for s in order]
    rings = [
        Ring(
            nz,
            z,
            lambda i, q=q: block(z2, i * tok, tok, q * feat, feat),
            lambda i, h, q=q: block(z2, i * tok, tok, q * feat + h * (feat // 2), feat // 2),
            zdev,
            *pair(),
        )
        for q in quarters
    ]
    rings.append(
        Ring(
            nz,
            z,
            lambda i: rows(z1, i * tok, tok),
            lambda i, h: block(z1, i * tok, tok, h * (feat // 2), feat // 2),
            zdev,
            *pair(),
        )
    )
    rings[0].step()
    rings[ny].step()
    info_z = go(
        Copies(nz, z, lambda i: rows(info, z * tok, tok), lambda m: rows(info, m * tok, tok), zdev, *pair())
    )
    tok2_y = go(Copies(ny, y, lambda i: tok2, lambda m: lanes(rows(z2, z * tok, tok), m, feat), ydev, *pair()))
    out_y = go(
        Copies(ny, y, lambda i: lanes(w_out.at[0], i, feat), lambda m: rows(wd, m * ff, ff), ydev, *pair())
    )

    def tick(some):
        for ring in some:
            ring.step()

    info_z.wait_recv()
    every = info[...]
    turned = every.T
    field = lambda base, k: turned[base + k : base + k + 1, :]
    expert_lane = iota((cols, 128), 1).astype(F32)
    tally = jnp.zeros((cols, 128), F32)
    for k in range(TOPK):
        tally += (every[:, E1 + k : E1 + k + 1] == expert_lane).astype(F32)
    counts[pl.ds(p * 8, 8), :] = jnp.broadcast_to(jnp.sum(tally, axis=0, keepdims=True), (8, 128))
    counts_p = go(
        Copies(npl, p, lambda i: rows(counts, p * 8, 8), lambda m: rows(counts, m * 8, 8), pdev, *pair())
    )
    tick([rings[0], rings[ny]])
    tok2_y.wait_recv()
    tick(rings[1:ny])

    def selection(match, length):
        number = dot(match.astype(BF16), earlier)
        slot = (iota((length, cols), 0) // nz % SLOT).astype(F32)
        return jnp.where(number == slot, match, 0.0)

    def sourced(length):
        return (iota((length, cols), 0) % nz) == (iota((length, cols), 1) // tok)

    same_z = sourced(chunk)
    match = jnp.zeros((chunk, cols), F32)
    gate = jnp.zeros((chunk, cols), F32)
    for k in range(TOPK):
        hit = (field(E1, k) == holder) & same_z
        match += hit.astype(F32)
        gate += jnp.where(hit, field(G1, k), 0.0)
    sel1 = selection(match, chunk)
    mixers = [(sel1 * gate).T]
    sel1 = sel1.astype(BF16)
    tick(rings)
    counts_p.wait_recv()
    total = counts[0:8, :]
    for other in range(1, npl):
        total += counts[other * 8 : other * 8 + 8, :]
    lane = iota((1, 128), 1)
    total = jnp.where(lane < nz * npl, total[0:1, :], -1.0)
    most = jnp.max(total, axis=1, keepdims=True)
    hot = jnp.min(jnp.where(total == most, lane.astype(F32), 1e6), axis=1, keepdims=True)

    match = jnp.zeros((chunk, cols), F32)
    gate = jnp.zeros((chunk, cols), F32)
    for k in range(TOPK):
        chosen, pick = field(E2, k), field(PICK, k)
        hit = (chosen == holder) & ((chosen != hot) | (pick == 0.0)) & same_z
        match += hit.astype(F32)
        gate += jnp.where(hit, field(G2, k), 0.0)
    sel2 = selection(match, chunk)
    mixer2 = (sel2 * gate).T
    sel2 = sel2.astype(BF16)
    tick(rings)

    rings[ny].finish()
    xs1[...] = dot(sel1, z1[...]).astype(BF16)
    mine = lambda ref: lanes(ref, y, feat)
    x1 = go(
        Copies(npl, p, lambda i: rows(xs1, i * s1, s1), lambda m: mine(rows(xr, m * s1, s1)), pdev, *pair())
    )
    xr[pl.ds(p * s1, s1), pl.ds(pl.multiple_of(y * feat, feat), feat)] = xs1[pl.ds(p * s1, s1), :]
    tick(rings[1:ny])

    hots = COPIES * s1
    copy_number = (iota((hots, cols), 0) // s1 + 1).astype(F32)
    same_copy = sourced(hots)
    match = jnp.zeros((hots, cols), F32)
    gate = jnp.zeros((hots, cols), F32)
    for k in range(TOPK):
        hit = (field(E2, k) == hot) & (field(PICK, k) == copy_number) & same_copy
        match += hit.astype(F32)
        gate += jnp.where(hit, field(G2, k), 0.0)
    selh = selection(match, hots)
    gated = selh * gate
    chip = z * nx + iota((chunk, here), 0) // s1
    on_chip = (home[0:1, :] // CORES == chip) & (iota((chunk, here), 0) < nx * s1)
    total = jnp.where(on_chip & (iota((chunk, here), 1).astype(F32) == hot), 1.0, 0.0)
    chip_hot = jnp.sum(total, axis=1, keepdims=True) > 0.0
    own = jnp.where((home[0:1, :] == e) & (iota((1, here), 1).astype(F32) == hot), 1.0, 0.0)
    own_hot = jnp.sum(own, axis=1, keepdims=True) > 0.0
    mixers.append(mixer2)
    for j in range(COPIES):
        tiled = jnp.concatenate([gated[j * s1 : (j + 1) * s1]] * npl, axis=0)
        mixers.append(jnp.where(chip_hot, tiled, 0.0).T)
    selh = selh.astype(BF16)

    def exchange(s):
        q = quarters[s]
        part = pl.ds(pl.multiple_of(q * feat, feat), feat)
        xs2[:, part] = dot(sel2, z2[:, part]).astype(BF16)
        copies = go(
            Copies(
                npl,
                p,
                lambda i: block(xs2, i * s1, s1, q * feat, feat),
                lambda m: block(xr, chunk + m * s1, s1, q * feat, feat),
                pdev,
                *pair(),
            )
        )
        xr[pl.ds(chunk + p * s1, s1), part] = xs2[pl.ds(p * s1, s1), part]
        return copies

    x2 = []
    for s in range(ny):
        rings[s].finish()
        x2.append(exchange(s))
        tick(rings[s + 1 : ny])

    hot_base = lambda j, i, core: (2 + j) * chunk + (core * nx + i) * s1
    hot_rings, siblings = [], []
    for j in range(COPIES):
        for s in range(ny):
            part = slice(s * feat, (s + 1) * feat)
            xr[pl.ds(hot_base(j, x, c), s1), part] = dot(selh[j * s1 : (j + 1) * s1], z2[:, part]).astype(BF16)
        hot_rings.append(
            Ring(
                nx,
                x,
                lambda i, j=j: rows(xr, hot_base(j, i, c), s1),
                lambda i, h, j=j: block(xr, hot_base(j, i, c), s1, h * (width // 2), width // 2),
                xdev,
                *pair(),
            )
        )
        siblings.append(([], *pair()))

    def to_sibling(j, i):
        items, send, recv = siblings[j]
        ref = rows(xr, hot_base(j, i, c), s1)
        item = pltpu.make_async_remote_copy(
            src_ref=ref,
            dst_ref=ref,
            send_sem=send.at[len(items)],
            recv_sem=recv.at[len(items)],
            device_id=pdev(x * CORES + 1 - c),
            device_id_type=MESH,
        )
        item.start()
        items.append(item)

    def hot_step(j):
        ring = hot_rings[j]
        k = ring.at
        ring.step()
        if k == 0:
            to_sibling(j, x)
        elif k < ring.steps:
            to_sibling(j, lax.rem(x + nx - k, nx))
            to_sibling(j, lax.rem(x + k, nx))
        else:
            to_sibling(j, lax.rem(x + k, nx))

    def hot_arrived(j):
        while hot_rings[j].at <= hot_rings[j].steps:
            hot_step(j)
        for item in siblings[j][0]:
            item.wait_recv()

    def front(i):
        part = pl.ds(i * chunk, chunk)
        acc[...] = jnp.zeros_like(acc)

        @pl.loop(0, ny)
        def _(q):
            features = pl.ds(pl.multiple_of(q * feat, feat), feat)
            a = xr[part, features]
            for half in range(2):
                acc[:, half * ff : (half + 1) * ff] += dot(a, wgu[half, features, :])

        gated = acc[:, 0:ff]
        value = gated / (1.0 + jnp.exp(-gated)) * acc[:, ff : 2 * ff]
        hid[part, pl.ds(pl.multiple_of(y * ff, ff), ff)] = value.astype(BF16)
        ref = block(hid, i * chunk, chunk, y * ff, ff)
        return go(Copies(ny, y, lambda m: ref, lambda m: block(hid, i * chunk, chunk, m * ff, ff), ydev, *pair()))

    def back(i, gathered):
        gathered.wait_recv()
        part = pl.ds(i * chunk, chunk)
        o[part, :] = dot(hid[part, :], wd[...]).astype(BF16)
        own = pl.ds(i * chunk + p * s1, s1)
        ro[own, :] = o[own, :]
        return go(
            Copies(
                npl,
                p,
                lambda m: rows(o, i * chunk + m * s1, s1),
                lambda m: rows(ro, i * chunk + m * s1, s1),
                pdev,
                *pair(),
            )
        )

    def back_hot(i, gathered):
        gathered.wait_recv()
        part = pl.ds(i * chunk, chunk)
        o[part, :] = jnp.where(own_hot, dot(hid[part, :], wd[...]), 0.0).astype(BF16)
        half = nx * s1
        away = rows(o, i * chunk + (1 - c) * half, half)
        item = pltpu.make_async_remote_copy(
            src_ref=away,
            dst_ref=rows(halves, (i - 2) * half, half),
            send_sem=half_send.at[i - 2],
            recv_sem=half_recv.at[i - 2],
            device_id=pdev(x * CORES + 1 - c),
            device_id_type=MESH,
        )
        item.start()
        siblings.append(([item], None, None))
        return item

    def back_chip(i, item):
        item.wait_recv()
        half = nx * s1
        kept = pl.ds(i * chunk + c * half, half)
        o[kept, :] += halves[pl.ds((i - 2) * half, half), :]
        own = pl.ds(i * chunk + x * s1, s1)
        ro[own, :] = o[pl.ds(i * chunk + c * half + x * s1, s1), :]
        return go(
            Copies(
                nx,
                x,
                lambda m: rows(o, i * chunk + c * half + m * s1, s1),
                lambda m: rows(ro, i * chunk + m * s1, s1),
                xdev,
                *pair(),
            )
        )

    def mixed(i, returned):
        returned.wait_recv()
        high = mixers[i].astype(BF16)
        low = (mixers[i] - high.astype(F32)).astype(BF16)
        used = nx * s1 if i > 1 else chunk
        both = jnp.concatenate([high[:, 0:used], low[:, 0:used]], axis=0)
        sums = dot(both, ro[pl.ds(i * chunk, used), :])
        return sums[0:cols] + sums[cols:]

    def deliver(b):
        copies = go(
            Copies(
                nz,
                z,
                lambda m: rows(mix, b * cols + m * tok, tok),
                lambda m: rows(inbox, b * cols + m * tok, tok),
                zdev,
                *pair(),
            )
        )
        own = pl.ds(b * cols + z * tok, tok)
        inbox[own, :] = mix[own, :]
        return copies

    def final(b, copies):
        copies.wait_recv()
        total = inbox[b * cols : b * cols + tok, :].astype(F32)
        for i in range(1, nz):
            start = b * cols + i * tok
            total += inbox[start : start + tok, :].astype(F32)
        out[b * tok : (b + 1) * tok, :] = total

    half_send, half_recv = pair()
    hot_step(0)
    hot_step(1)
    x1.wait_recv()
    y1 = go(Copies(ny, y, lambda i: mine(rows(xr, 0, chunk)), lambda m: lanes(rows(xr, 0, chunk), m, feat), ydev, *pair()))

    weights.wait()
    for copies in x2:
        copies.wait_recv()
    h1 = front(1)
    hot_step(0)
    hot_step(2)
    hot_step(1)
    hot_arrived(0)
    h2 = front(2)
    hot_step(2)
    own_out.wait()
    out_y.wait_recv()
    r1 = back(1, h1)
    hot_arrived(1)
    h3 = front(3)
    b2 = back_hot(2, h2)
    hot_arrived(2)
    h4 = front(4)
    r2 = back_chip(2, b2)
    b3 = back_hot(3, h3)
    y1.wait_recv()
    h0 = front(0)
    r3 = back_chip(3, b3)
    b4 = back_hot(4, h4)
    blend[...] = mixed(1, r1)
    r4 = back_chip(4, b4)
    r0 = back(0, h0)
    blend[...] += mixed(2, r2)
    blend[...] += mixed(3, r3)
    mix[cols : 2 * cols, :] = (blend[...] + mixed(4, r4)).astype(BF16)
    d2 = deliver(1)
    mix[0:cols, :] = mixed(0, r0).astype(BF16)
    d1 = deliver(0)
    final(1, d2)
    final(0, d1)

    for copies in started + rings + hot_rings:
        copies.wait_send()
    for items, _, _ in siblings:
        for item in items:
            item.wait_send()


def shards(
    dims, tokens_one, experts_one, gates_one, tokens_two, experts_two, gates_two, replica_pick, home, w_gate_up, w_down
):
    nz, nx, ny = dims
    npl = nx * CORES
    tok, feat = tokens_one.shape
    width = feat * ny
    ff = w_gate_up.shape[3]
    cols = nz * tok
    chunk = npl * SLOT * nz
    chunks = 2 + COPIES
    vmem = pltpu.VMEM
    dma = pltpu.SemaphoreType.DMA
    size = max(nz, npl, ny, nx) + 4
    groups = 1 + 2 + ny + 2 + 1 + 1 + 2 + ny + 2 * COPIES + 1 + 1 + 2 * chunks + 2
    any_spec = pl.BlockSpec(memory_space=pl.ANY)
    in_vmem = pl.BlockSpec(memory_space=pltpu.VMEM)
    out = pl.pallas_call(
        functools.partial(kernel, dims),
        out_shape=jax.ShapeDtypeStruct((2 * tok, feat), F32),
        in_specs=[in_vmem] * 8 + [any_spec] * 2,
        out_specs=in_vmem,
        scratch_shapes=[
            vmem((128, 128), F32),
            vmem((cols, 128), F32),
            vmem((npl * 8, 128), F32),
            vmem((cols, feat), BF16),
            vmem((cols, width), BF16),
            vmem((chunk, feat), BF16),
            vmem((chunk, width), BF16),
            vmem((chunks * chunk, width), BF16),
            vmem((chunk, 2 * ff), F32),
            vmem((chunks * chunk, ff * ny), BF16),
            vmem((chunks * chunk, feat), BF16),
            vmem((chunks * chunk, feat), BF16),
            vmem((cols, feat), F32),
            vmem((2 * cols, feat), BF16),
            vmem((2 * cols, feat), BF16),
            vmem((COPIES * nx * SLOT * nz, feat), BF16),
            vmem(w_gate_up.shape[1:], BF16),
            vmem((ff * ny, feat), BF16),
            dma((2,)),
        ]
        + [dma((size,)) for _ in range(2 * groups)],
        compiler_params=pltpu.CompilerParams(
            collective_id=0, has_side_effects=True, vmem_limit_bytes=56 * 1024 * 1024
        ),
        cost_estimate=pl.CostEstimate(flops=10_000_000_000, bytes_accessed=16_000_000, transcendentals=0),
    )(
        tokens_one,
        tokens_two,
        experts_one.T,
        gates_one.T,
        experts_two.T,
        gates_two.T,
        replica_pick.T,
        home[None, :],
        w_gate_up,
        w_down,
    )
    return out[:tok].astype(BF16), out[tok:].astype(BF16)


def solution(mesh):
    placed = (
        P("expert", "inner"),
        P("expert", None),
        P("expert", None),
        P("expert", "inner"),
        P("expert", None),
        P("expert", None),
        P("expert", None),
        P(),
        P("expert", None, None, "inner"),
        P("expert", "inner", None),
    )
    experts, inner = mesh.shape["expert"], mesh.shape["inner"]
    nx = 4 if experts >= 16 else 2
    dims = (experts // (nx * CORES), nx, inner)
    return jax.shard_map(
        functools.partial(shards, dims),
        mesh=mesh,
        in_specs=placed,
        out_specs=(P("expert", "inner"), P("expert", "inner")),
        check_vma=False,
    )
```

time: 158 us -> 135 us (0.85)
  Pallas kernels: 149 us -> 133 us
  local copies, waits for them, and re-layouts: 7.24 us -> 0.65 us
    pallas_call x1, Pallas kernels: 149 us -> 133 us  [shards(): pl.pallas_call(functools.partial(kernel, dims), out_shape=jax.ShapeDtypeS...]
    unnamed x5 -> x0, local copies, waits for them, and re-layouts: 5.16 us -> none
where the time goes in v2:
time: 135 us
  Pallas kernels  133 us (99%)
    pallas_call x1, Pallas kernels, shards(): pl.pallas_call(functools.partial(kernel, dims), out_shape=jax.ShapeDtypeS...  133 us

profile of v2, /device:TPU:1, one launch (start us, length us, event | category | flops | bytes accessed | tf_op | source)
XLA Modules:
  0.0 134.8 jit_solution(18076202375955723184)
XLA Ops:
  0.6 132.5 %shard_map.113 = f32[32,1792]{1,0:T(8,128)} custom-call(bf16[16,1792]{1,0:T(8,128)(2,1)} %tok1.1, bf16[16,1792]{1,0:T(8,128)(2,1)} %tok2.1, s32[8,16]{1,0:T(8,128)} %bitcast.6, f32[8,16]{1,0:T(8,128)} %bitcast.7, s32[8,16]{1,0:T(8,128)} %bitcast.8, f32[8,16]{1,0:T(8,128)} %bitcast.9, s32[8,16]{1,0:T(8,128)} %bitcast.10, s32[1,64]{1,0:T(1,128)} %bitcast.11, ...), custom_call_target="tpu_custom_call" | custom-call | flops 10000000000 | bytes 16000000 | tf_op jit(solution)/shard_map/pallas_call | solution.py:576
  133.2 1.0 convert.4
  134.1 0.6 fusion

commit v3 on v2

--- a/solution.py
+++ b/solution.py
@@ -230,19 +230,22 @@
             *pair(),
         )
     )
+    tok2_y = go(Copies(ny, y, lambda i: tok2, lambda m: lanes(rows(z2, z * tok, tok), m, feat), ydev, *pair()))
     rings[0].step()
     rings[ny].step()
     info_z = go(
         Copies(nz, z, lambda i: rows(info, z * tok, tok), lambda m: rows(info, m * tok, tok), zdev, *pair())
     )
-    tok2_y = go(Copies(ny, y, lambda i: tok2, lambda m: lanes(rows(z2, z * tok, tok), m, feat), ydev, *pair()))
-    out_y = go(
-        Copies(ny, y, lambda i: lanes(w_out.at[0], i, feat), lambda m: rows(wd, m * ff, ff), ydev, *pair())
-    )
 
     def tick(some):
         for ring in some:
             ring.step()
+
+    tok2_y.wait_recv()
+    tick(rings[1:ny])
+    out_y = go(
+        Copies(ny, y, lambda i: lanes(w_out.at[0], i, feat), lambda m: rows(wd, m * ff, ff), ydev, *pair())
+    )
 
     info_z.wait_recv()
     every = info[...]
@@ -257,8 +260,6 @@
         Copies(npl, p, lambda i: rows(counts, p * 8, 8), lambda m: rows(counts, m * 8, 8), pdev, *pair())
     )
     tick([rings[0], rings[ny]])
-    tok2_y.wait_recv()
-    tick(rings[1:ny])
 
     def selection(match, length):
         number = dot(match.astype(BF16), earlier)
@@ -526,28 +527,28 @@
     own_out.wait()
     out_y.wait_recv()
     r1 = back(1, h1)
+    y1.wait_recv()
+    h0 = front(0)
     hot_arrived(1)
     h3 = front(3)
     b2 = back_hot(2, h2)
+    r0 = back(0, h0)
+    r2 = back_chip(2, b2)
     hot_arrived(2)
     h4 = front(4)
-    r2 = back_chip(2, b2)
+    blend[...] = mixed(1, r1)
     b3 = back_hot(3, h3)
-    y1.wait_recv()
-    h0 = front(0)
+    mix[0:cols, :] = mixed(0, r0).astype(BF16)
+    d1 = deliver(0)
     r3 = back_chip(3, b3)
     b4 = back_hot(4, h4)
-    blend[...] = mixed(1, r1)
+    blend[...] += mixed(2, r2)
     r4 = back_chip(4, b4)
-    r0 = back(0, h0)
-    blend[...] += mixed(2, r2)
     blend[...] += mixed(3, r3)
     mix[cols : 2 * cols, :] = (blend[...] + mixed(4, r4)).astype(BF16)
     d2 = deliver(1)
-    mix[0:cols, :] = mixed(0, r0).astype(BF16)
-    d1 = deliver(0)
+    final(0, d1)
     final(1, d2)
-    final(0, d1)
 
     for copies in started + rings + hot_rings:
         copies.wait_send()

time: 135 us -> 130 us (0.963)
  Pallas kernels: 133 us -> 127 us
    pallas_call x1, Pallas kernels: 133 us -> 127 us  [shards(): pl.pallas_call(functools.partial(kernel, dims), out_shape=jax.ShapeDtypeS...]
where the time goes in v3:
time: 130 us; the launch traced here: 129 us
  Pallas kernels  127 us (98%)
    pallas_call x1, Pallas kernels, shards(): pl.pallas_call(functools.partial(kernel, dims), out_shape=jax.ShapeDtypeS...  127 us

profile of v3, /device:TPU:1, one launch (start us, length us, event | category | flops | bytes accessed | tf_op | source)
XLA Modules:
  0.0 129.5 jit_solution(12671819129664000767)
XLA Ops:
  0.6 127.2 %shard_map.113 = f32[32,1792]{1,0:T(8,128)} custom-call(bf16[16,1792]{1,0:T(8,128)(2,1)} %tok1.1, bf16[16,1792]{1,0:T(8,128)(2,1)} %tok2.1, s32[8,16]{1,0:T(8,128)} %bitcast.6, f32[8,16]{1,0:T(8,128)} %bitcast.7, s32[8,16]{1,0:T(8,128)} %bitcast.8, f32[8,16]{1,0:T(8,128)} %bitcast.9, s32[8,16]{1,0:T(8,128)} %bitcast.10, s32[1,64]{1,0:T(1,128)} %bitcast.11, ...), custom_call_target="tpu_custom_call" | custom-call | flops 10000000000 | bytes 16000000 | tf_op jit(solution)/shard_map/pallas_call | solution.py:577
  127.9 1.0 convert.4
  128.8 0.6 fusion

commit v4 on v3

--- a/solution.py
+++ b/solution.py
@@ -485,28 +485,75 @@
         sums = dot(both, ro[pl.ds(i * chunk, used), :])
         return sums[0:cols] + sums[cols:]
 
-    def deliver(b):
-        copies = go(
-            Copies(
-                nz,
-                z,
-                lambda m: rows(mix, b * cols + m * tok, tok),
-                lambda m: rows(inbox, b * cols + m * tok, tok),
-                zdev,
-                *pair(),
+    def block_for(b, ahead):
+        return pl.ds(b * cols + lax.rem(z + ahead + nz, nz) * tok, tok)
+
+    def slot(b, k):
+        return pl.ds(b * cols + k * tok, tok)
+
+    class Sums:
+        def __init__(self, b):
+            self.b = b
+            self.sems = pair()
+            self.items = []
+            inbox[slot(b, 0), :] = mix[block_for(b, 0), :]
+            whole, low, high = pl.ds(0, feat), pl.ds(0, feat // 2), pl.ds(feat // 2, feat // 2)
+            if nz == 8:
+                self.send(-1, -1, 1, whole)
+                self.send(1, 1, 2, whole)
+                self.send(-1, -3, 5, whole)
+                self.send(1, 3, 6, whole)
+                self.send(-2, -4, 7, low)
+                self.send(2, 4, 7, high)
+            else:
+                for i in range(1, nz):
+                    self.send(i, i, i, whole)
+
+        def send(self, step, ahead, k, part):
+            i = len(self.items)
+            send, recv = self.sems
+            item = pltpu.make_async_remote_copy(
+                src_ref=mix.at[block_for(self.b, ahead), part],
+                dst_ref=inbox.at[slot(self.b, k), part],
+                send_sem=send.at[i],
+                recv_sem=recv.at[i],
+                device_id=zdev(lax.rem(z + step + nz, nz)),
+                device_id_type=MESH,
             )
-        )
-        own = pl.ds(b * cols + z * tok, tok)
-        inbox[own, :] = mix[own, :]
-        return copies
-
-    def final(b, copies):
-        copies.wait_recv()
-        total = inbox[b * cols : b * cols + tok, :].astype(F32)
-        for i in range(1, nz):
-            start = b * cols + i * tok
-            total += inbox[start : start + tok, :].astype(F32)
-        out[b * tok : (b + 1) * tok, :] = total
+            item.start()
+            self.items.append(item)
+
+        def relay(self):
+            if nz != 8:
+                return
+            for item in self.items[2:6]:
+                item.wait_recv()
+            b, half = self.b, feat // 2
+            for ahead, k in ((-2, 5), (2, 6)):
+                total = mix[block_for(b, ahead), :].astype(F32) + inbox[slot(b, k), :].astype(F32)
+                opposite = inbox[slot(b, 7), :].astype(F32)
+                nearer = iota((tok, feat), 1) < half if ahead < 0 else iota((tok, feat), 1) >= half
+                mix[block_for(b, ahead), :] = (total + jnp.where(nearer, opposite, 0.0)).astype(BF16)
+            whole = pl.ds(0, feat)
+            self.send(-2, -2, 3, whole)
+            self.send(2, 2, 4, whole)
+
+        def finish(self):
+            b = self.b
+            if nz == 8:
+                for item in self.items[:2] + self.items[6:]:
+                    item.wait_recv()
+            else:
+                for item in self.items:
+                    item.wait_recv()
+            total = inbox[slot(b, 0), :].astype(F32)
+            for k in range(1, 5 if nz == 8 else nz):
+                total += inbox[slot(b, k), :].astype(F32)
+            out[b * tok : (b + 1) * tok, :] = total
+
+        def wait_send(self):
+            for item in self.items:
+                item.wait_send()
 
     half_send, half_recv = pair()
     hot_step(0)
@@ -539,18 +586,20 @@
     blend[...] = mixed(1, r1)
     b3 = back_hot(3, h3)
     mix[0:cols, :] = mixed(0, r0).astype(BF16)
-    d1 = deliver(0)
+    d1 = Sums(0)
     r3 = back_chip(3, b3)
     b4 = back_hot(4, h4)
     blend[...] += mixed(2, r2)
     r4 = back_chip(4, b4)
     blend[...] += mixed(3, r3)
+    d1.relay()
     mix[cols : 2 * cols, :] = (blend[...] + mixed(4, r4)).astype(BF16)
-    d2 = deliver(1)
-    final(0, d1)
-    final(1, d2)
-
-    for copies in started + rings + hot_rings:
+    d2 = Sums(1)
+    d2.relay()
+    d1.finish()
+    d2.finish()
+
+    for copies in started + rings + hot_rings + [d1, d2]:
         copies.wait_send()
     for items, _, _ in siblings:
         for item in items:

time: 130 us -> 127 us (0.977)
  Pallas kernels: 127 us -> 124 us
    pallas_call x1, Pallas kernels: 127 us -> 124 us  [shards(): pl.pallas_call(functools.partial(kernel, dims), out_shape=jax.ShapeDtypeS...]
where the time goes in v4:
time: 127 us
  Pallas kernels  124 us (98%)
    pallas_call x1, Pallas kernels, shards(): pl.pallas_call(functools.partial(kernel, dims), out_shape=jax.ShapeDtypeS...  124 us

profile of v4, /device:TPU:1, one launch (start us, length us, event | category | flops | bytes accessed | tf_op | source)
XLA Modules:
  0.0 126.6 jit_solution(14303640639541846867)
XLA Ops:
  0.6 124.3 %shard_map.113 = f32[32,1792]{1,0:T(8,128)} custom-call(bf16[16,1792]{1,0:T(8,128)(2,1)} %tok1.1, bf16[16,1792]{1,0:T(8,128)(2,1)} %tok2.1, s32[8,16]{1,0:T(8,128)} %bitcast.6, f32[8,16]{1,0:T(8,128)} %bitcast.7, s32[8,16]{1,0:T(8,128)} %bitcast.8, f32[8,16]{1,0:T(8,128)} %bitcast.9, s32[8,16]{1,0:T(8,128)} %bitcast.10, s32[1,64]{1,0:T(1,128)} %bitcast.11, ...), custom_call_target="tpu_custom_call" | custom-call | flops 10000000000 | bytes 16000000 | tf_op jit(solution)/shard_map/pallas_call | solution.py:626
  125.0 1.0 convert.4
  125.9 0.6 fusion

commit v5 on v4

--- a/solution.py
+++ b/solution.py
@@ -561,12 +561,12 @@
     x1.wait_recv()
     y1 = go(Copies(ny, y, lambda i: mine(rows(xr, 0, chunk)), lambda m: lanes(rows(xr, 0, chunk), m, feat), ydev, *pair()))
 
+    hot_step(2)
     weights.wait()
     for copies in x2:
         copies.wait_recv()
+    hot_step(0)
     h1 = front(1)
-    hot_step(0)
-    hot_step(2)
     hot_step(1)
     hot_arrived(0)
     h2 = front(2)

time: 127 us -> 129 us (1.016)
  Pallas kernels: 124 us -> 127 us
    pallas_call x1, Pallas kernels: 124 us -> 127 us  [shards(): pl.pallas_call(functools.partial(kernel, dims), out_shape=jax.ShapeDtypeS...]
where the time goes in v5:
time: 129 us
  Pallas kernels  127 us (98%)
    pallas_call x1, Pallas kernels, shards(): pl.pallas_call(functools.partial(kernel, dims), out_shape=jax.ShapeDtypeS...  127 us

profile of v5, /device:TPU:1, one launch (start us, length us, event | category | flops | bytes accessed | tf_op | source)
XLA Modules:
  0.0 129.3 jit_solution(842842882603616723)
XLA Ops:
  0.6 127.0 %shard_map.113 = f32[32,1792]{1,0:T(8,128)} custom-call(bf16[16,1792]{1,0:T(8,128)(2,1)} %tok1.1, bf16[16,1792]{1,0:T(8,128)(2,1)} %tok2.1, s32[8,16]{1,0:T(8,128)} %bitcast.6, f32[8,16]{1,0:T(8,128)} %bitcast.7, s32[8,16]{1,0:T(8,128)} %bitcast.8, f32[8,16]{1,0:T(8,128)} %bitcast.9, s32[8,16]{1,0:T(8,128)} %bitcast.10, s32[1,64]{1,0:T(1,128)} %bitcast.11, ...), custom_call_target="tpu_custom_call" | custom-call | flops 10000000000 | bytes 16000000 | tf_op jit(solution)/shard_map/pallas_call | solution.py:626
  127.7 1.0 convert.4
  128.6 0.6 fusion
